TPU v7x, 256 devices: a whole 4x4x8 slice. The times are simulated.
256 devices in a mesh: role: 4 (over z_hi), slab: 64 (over z_lo, y, x, core).
Axes of the slice: x: 4, y: 4, z: 8 (z_hi: 4, z_lo: 2; z = z_hi * 2 + z_lo), core: 2. Of those that a mesh axis runs over, the one named last changes fastest.
Arguments:
- velocity: float32 [3, 32, 4096, 128], P(None, 'role', 'slab'), may hold values from -6 to 6
- anchors: int32 [64, 2], P('slab'), may hold values from 0 to 32
- slot_table: int32 [64, 2], P('slab'), may hold values from -1 to 63, as said below
- lift: float32 [3, 64], replicated, may hold values from -3.5 to 3.5
- mix: float32 [64, 64], replicated, may hold values from -0.75 to 0.75
- proj: float32 [3, 64], replicated, may hold values from -0.75 to 0.75
- spectral: float32 [4096, 64, 64], P(('role', 'slab')), may hold values from -0.75 to 0.75
Outputs:
- advanced: float32 [3, 32, 4096, 128], P(None, 'role', 'slab')
- patch_loss: float32 [64, 2], P('slab')
- grad_lift: float32 [3, 64], replicated
- grad_mix: float32 [64, 64], replicated
- grad_proj: float32 [3, 64], replicated
- grad_spectral: float32 [4096, 64, 64], P(('role', 'slab'))
Inputs may be any that keep to these rules, and one draw needn't show every extreme that they name: anchors[g] gives the x and y offsets of patch g inside the slab of device g. `slot_table`: row t lists the patches that trainer t takes, -1 marking an empty slot; every patch index from 0 to 63 stands exactly once in the table, and at least one row is full.
All inputs are finite; a program needn't handle non-finite values.
Results may differ from a plain program's by a relative error of at most 0.0025.
Values may be sent and summed in bfloat16 or wider, within the bound.
A program may use at most 128 MiB of HBM per device.

v0:
```python
import math

import jax
import jax.numpy as jnp
import numpy as np
from jax import lax
from jax.experimental import pallas as pl
from jax.experimental.pallas import tpu as pltpu
from jax.sharding import PartitionSpec as P

MODES = 16
PATCH = 32
AREA = PATCH * PATCH
ROLES = 4
SLABS = 64
YX = 16
CREW = 16
PLANES = 8
WIDTH = 64
PART = WIDTH // ROLES
SH = 4
TILE = 128
PAIRS = 3 * PLANES

time_step = 0.1
viscosity = 1.5
tiny_eps = 1e-06
exact = lax.Precision.HIGHEST
MESH = pl.DeviceIdType.MESH
root = math.sqrt(2.0 / math.pi)
NN = (((1,), (0,)), ((), ()))
NT = (((1,), (1,)), ((), ()))
TN = (((0,), (0,)), ((), ()))


def dot(a, b, dims=NN):
    return lax.dot_general(a, b, dims, precision=exact, preferred_element_type=jnp.float32)


def split(value):
    high = value.astype(jnp.bfloat16)
    return high, (value - high.astype(jnp.float32)).astype(jnp.bfloat16)


def pass_(a, b, dims):
    return lax.dot_general(a, b, dims, preferred_element_type=jnp.float32)


def dot3(a, b, dims=NN):
    return pass_(a[0], b[0], dims) + (pass_(a[0], b[1], dims) + pass_(a[1], b[0], dims))


def dot2(a, exact_b, dims=NN):
    return pass_(a[0], exact_b, dims) + pass_(a[1], exact_b, dims)


def fourier_table():
    order = np.arange(MODES)[:, None]
    points = np.arange(PATCH)[None, :]
    angles = 2.0 * math.pi * ((order + 1) // 2) * points / PATCH
    waves = np.where((order % 2 == 1) | (order == 0), np.cos(angles), np.sin(angles))
    return waves * np.where(order == 0, math.sqrt(1.0 / PATCH), math.sqrt(2.0 / PATCH))


def pair(table):
    table = table.astype(np.float32)
    high = table.astype(jnp.bfloat16)
    return jnp.asarray(np.stack([high, (table - high.astype(np.float32)).astype(jnp.bfloat16)]))


def tables():
    phi = fourier_table()
    over_x = phi.reshape(2, 4, 2, 4, 8)
    over_y = phi.reshape(2, 8, PATCH)
    plane = np.einsum("axchl,gky->gcaxklhy", over_x, over_y).reshape(256, AREA)
    phi_z = phi.reshape(ROLES, SH, ROLES, PLANES)
    eye2, eye3, eye4, eye16 = np.eye(2), np.eye(3), np.eye(ROLES), np.eye(PART)
    ones = np.ones(PART)
    spread = np.einsum("hg,rsbz,ij,c->hbzijsgrc", eye2, phi_z, eye3, ones).reshape(2 * ROLES * PAIRS, 3 * SH * TILE)
    short = np.einsum("hg,rsbz,ij->hbzisjgr", eye2, phi_z, eye3).reshape(2 * ROLES * PAIRS, SH, 24)
    short = np.pad(short, ((0, 0), (0, 0), (0, TILE - 24))).reshape(-1, SH * TILE)
    inverse = np.einsum("hg,rsbz,cd->bhzcsgrd", eye2, phi_z, eye16).reshape(ROLES * 256, SH * TILE)
    expand = np.einsum("ij,hg,rs,c->ihrjgsc", eye3, eye2, eye4, ones).reshape(24, 3 * TILE)
    expand = np.pad(expand, ((0, TILE - 24), (0, 0)))
    sort = np.einsum("ij,hg,rs,cd->ihrcsjgd", eye3, eye2, eye4, eye16).reshape(3 * TILE, ROLES, 96)
    sort = np.pad(sort, ((0, 0), (0, 0), (0, TILE - 96))).reshape(3 * TILE, ROLES * TILE)
    return [pair(plane), pair(np.concatenate([spread, short], axis=1)), pair(inverse), jnp.asarray(expand, jnp.bfloat16), jnp.asarray(sort, jnp.bfloat16)]


def place(team, slab):
    return team // 2 * 32 + slab % 32 // 2 * 2 + team % 2


ROWS = 96


def step_kernel(
    anchors, vel, spectral_in, lift_in, mix_in, proj_in, plane_in, spread_in, inverse_in, expand_in, sort_in,
    second_out, raw_out, tile_out,
    ext, mid, after_two, spectral, lift, mix, proj, plane, spread, inverse, expand, sort,
    w_send, w_in, w_all, cut_out, cut_in, a_rows, t_rows, bands, a_send, a_got, a_wide, y_send, y_got,
    seen_wide, proj_wide, act, slope, g_high, g_low, out_sum, twice, g_send, g_got, m_send, m_got, r_send, r_got, raw,
    s_crew, s_yx,
    local_sem, z_sem, x_sem, c_sem, cross_sem, swap_sem, wy_sem, band_sem, y_sem, g_sem, a_sem, m_sem, back_sem,
    sc_sem, sy_sem,
):
    role, slab = lax.axis_index("role"), lax.axis_index("slab")
    yx = slab % 32 // 2
    team = slab // 32 * 2 + slab % 2
    patch = role // 2 * 32 + yx * 2 + role % 2
    after, before = (slab + 1) % SLABS, (slab + SLABS - 1) % SLABS
    teams = [(d, (team + d) % ROLES) for d in range(1, ROLES)]
    crew = [(d, (role * ROLES + team + d) % CREW) for d in range(1, CREW)]
    spots = [(d, (yx + d) % YX) for d in range(1, YX)]
    home = role == team
    pending = []

    def remote(src, dst, send_sem, recv_sem, to_role, to_slab):
        return pltpu.make_async_remote_copy(
            src_ref=src, dst_ref=dst, send_sem=send_sem, recv_sem=recv_sem,
            device_id=(to_role, to_slab), device_id_type=MESH,
        )

    def to_spot(at):
        return slab // 32 * 32 + at * 2 + slab % 2

    def send(src, dst, sems, d, to_role, to_slab):
        copy = remote(src, dst, sems.at[0, d], sems.at[1, d], to_role, to_slab)
        copy.start()
        pending.append(copy)
        return copy

    def fetch(at, src, dst):
        copy = pltpu.make_async_copy(src, dst, local_sem.at[at])
        copy.start()
        return copy

    own = fetch(0, vel, ext.at[:, pl.ds(2, PLANES), pl.ds(16, 64)])
    fetched = [fetch(1, spectral_in, spectral), fetch(2, lift_in, lift), fetch(3, mix_in, mix), fetch(4, proj_in, proj)]
    later = [
        fetch(5, plane_in, plane), fetch(6, spread_in, spread), fetch(7, inverse_in, inverse), fetch(8, expand_in, expand),
        fetch(9, sort_in, sort),
    ]

    barrier = pltpu.get_barrier_semaphore()

    def greet(to_role, to_slab):
        pl.semaphore_signal(barrier, inc=1, device_id=(to_role, to_slab), device_id_type=MESH)

    greet(role, after)
    greet(role, before)

    @pl.when(role > 0)
    def _():
        greet(role - 1, after)
        greet(role - 1, before)

    @pl.when(role < ROLES - 1)
    def _():
        greet(role + 1, after)
        greet(role + 1, before)

    for _, to in crew:
        greet(to // ROLES, place(to % ROLES, slab))
    for _, to in spots:
        greet(role, to_spot(to))

    source = lax.broadcasted_iota(jnp.int32, (ROLES * TILE, TILE), 0)
    target = lax.broadcasted_iota(jnp.int32, (ROLES * TILE, TILE), 1)
    pick = (
        (source // TILE == target % WIDTH // PART)
        & (source % TILE // WIDTH == target // WIDTH)
        & (source % WIDTH // PART == role)
        & (source % PART == target % PART)
    )
    pick = jnp.where(pick, 1.0, 0.0).astype(jnp.bfloat16)
    for copy in fetched:
        copy.wait()
    row_ky = lax.broadcasted_iota(jnp.int32, (MODES, MODES * WIDTH), 0)
    lane_ky = lax.broadcasted_iota(jnp.int32, (MODES, MODES * WIDTH), 1) // WIDTH
    twin = jnp.concatenate([lift[...], lift[...]], axis=1)
    long = jnp.concatenate([twin] * (MODES // 2), axis=1)
    blocks = [jnp.where(row_ky == lane_ky, long[i : i + 1], 0.0) for i in range(3)]
    lifted = dot3(
        split(jnp.concatenate(blocks, axis=0)), split(spectral[...].reshape(MODES * WIDTH, WIDTH))
    )
    lifted = lifted.reshape(3, 2, 8, WIDTH)
    lifted = jnp.concatenate([lifted[:, 0].reshape(24, WIDTH), lifted[:, 1].reshape(24, WIDTH)], axis=1)
    lifted = dot2(split(lifted), pick, NT)
    for k in range(ROLES):
        w_send[k] = lifted[:, k * TILE : (k + 1) * TILE].reshape(3, 8, TILE)

    pl.semaphore_wait(barrier, 34 + 2 * ((role + 1) // 2 % 2))

    def to_below(k):
        return remote(
            vel.at[:, pl.ds(k, 1)], ext.at[:, pl.ds(10 + k, 1), pl.ds(16, 64)],
            z_sem.at[0, k], z_sem.at[1, k], role - 1, slab,
        )

    def to_above(k):
        return remote(
            vel.at[:, pl.ds(7 - k, 1)], ext.at[:, pl.ds(1 - k, 1), pl.ds(16, 64)],
            z_sem.at[0, 2 + k], z_sem.at[1, 2 + k], role + 1, slab,
        )

    def corner(up, right, at):
        plane_at, slot = (7, 1) if up else (0, 10)
        row, spot = (56, 8) if right else (0, 80)
        return remote(
            vel.at[:, pl.ds(plane_at, 1), pl.ds(row, 8)], ext.at[:, pl.ds(slot, 1), pl.ds(spot, 8)],
            c_sem.at[0, at], c_sem.at[1, at], role + 1 if up else role - 1, after if right else before,
        )

    to_after = remote(
        vel.at[:, :, pl.ds(56, 8)], ext.at[:, pl.ds(2, PLANES), pl.ds(8, 8)],
        x_sem.at[0, 0], x_sem.at[1, 0], role, after,
    )
    to_before = remote(
        vel.at[:, :, pl.ds(0, 8)], ext.at[:, pl.ds(2, PLANES), pl.ds(80, 8)],
        x_sem.at[0, 1], x_sem.at[1, 1], role, before,
    )

    @pl.when(role > 0)
    def _():
        to_below(0).start()
        corner(False, True, 0).start()
        corner(False, False, 1).start()

    @pl.when(role < ROLES - 1)
    def _():
        to_above(0).start()
        corner(True, True, 2).start()
        corner(True, False, 3).start()

    to_after.start()
    to_before.start()

    o_copies = [
        send(w_send.at[to % ROLES], w_in.at[team, role], cross_sem, d, to // ROLES, place(to % ROLES, slab))
        for d, to in crew
    ]
    w_in[team, role] = w_send[team]

    @pl.when(role > 0)
    def _():
        to_below(1).start()

    @pl.when(role < ROLES - 1)
    def _():
        to_above(1).start()

    @pl.when(role == 0)
    def _():
        ext[:, pl.ds(0, 2)] = jnp.zeros((3, 2, ROWS, TILE), jnp.float32)

    @pl.when(role == ROLES - 1)
    def _():
        ext[:, pl.ds(10, 2)] = jnp.zeros((3, 2, ROWS, TILE), jnp.float32)

    seen = dot(mix[...], lift[...], (((0,), (1,)), ((), ())))
    unit = jnp.where(
        lax.broadcasted_iota(jnp.int32, (3, 3), 0) == lax.broadcasted_iota(jnp.int32, (3, 3), 1), 1.0, 0.0
    )
    proj_t = dot(proj[...], unit, TN)
    lift_t = dot(lift[...], unit, TN)
    for i in range(3):
        seen_wide[i] = jnp.broadcast_to(seen[:, i : i + 1], (WIDTH, TILE))
        proj_wide[i] = jnp.broadcast_to(proj_t[:, i : i + 1], (WIDTH, TILE))

    lane_80 = lax.broadcasted_iota(jnp.int32, (80, TILE), 1)
    lane_64 = lax.broadcasted_iota(jnp.int32, (64, TILE), 1)

    def advance(field, z, row, count, lane):
        centre = [field[c, z, pl.ds(row, count)] for c in range(3)]
        out = []
        for c in range(3):
            here = centre[c]
            z_next, z_prev = field[c, z + 1, pl.ds(row, count)], field[c, z - 1, pl.ds(row, count)]
            x_next, x_prev = field[c, z, pl.ds(row + 1, count)], field[c, z, pl.ds(row - 1, count)]
            y_next = jnp.where(lane == TILE - 1, 0.0, pltpu.roll(here, TILE - 1, 1))
            y_prev = jnp.where(lane == 0, 0.0, pltpu.roll(here, 1, 1))
            laplace = z_next + z_prev + x_next + x_prev + y_next + y_prev - 6.0 * here
            carried = 0.5 * (
                centre[0] * (z_next - z_prev) + centre[1] * (x_next - x_prev) + centre[2] * (y_next - y_prev)
            )
            out.append(here + time_step * (viscosity * laplace - carried))
        return out

    own.wait()
    to_after.wait_recv()
    to_before.wait_recv()

    def inner(z, carry):
        out = advance(ext, z, 8, 80, lane_80)
        for c in range(3):
            mid[c, z, pl.ds(8, 80)] = out[c]
        return carry

    lax.fori_loop(3, 9, inner, 0)

    @pl.when(role > 0)
    def _():
        to_above(0).wait_recv()
        corner(True, True, 2).wait_recv()
        corner(True, False, 3).wait_recv()

    @pl.when(role < ROLES - 1)
    def _():
        to_below(0).wait_recv()
        corner(False, True, 0).wait_recv()
        corner(False, False, 1).wait_recv()

    inner(2, 0)
    inner(9, 0)

    x_at, y_at = anchors[0, 0], anchors[0, 1]
    from_lane = lax.broadcasted_iota(jnp.int32, (TILE, TILE), 0)
    to_lane = lax.broadcasted_iota(jnp.int32, (TILE, TILE), 1)
    chosen = [
        jnp.where((from_lane == to_lane % PATCH + y_at) & (to_lane // PATCH == k), 1.0, 0.0).astype(jnp.bfloat16)
        for k in range(4)
    ]

    def cut(field, first_row, first_plane, at):
        total = None
        for k in range(4):
            rows = [
                field[c, z + first_plane, pl.ds(first_row + x_at + 8 * k, 8), :]
                for z in range(PLANES)
                for c in range(3)
            ]
            part = pass_(jnp.concatenate(rows, axis=0).astype(jnp.bfloat16), chosen[k], NN)
            total = part if total is None else total + part
        cut_out[at] = total.astype(jnp.bfloat16).reshape(12, 16, TILE)

    def swap(at):
        return remote(
            cut_out.at[at], cut_in.at[at], swap_sem.at[0, at], swap_sem.at[1, at], team, place(role, slab)
        )

    def swap_start(at):
        @pl.when(jnp.logical_not(home))
        def _():
            swap(at).start()

        @pl.when(home)
        def _():
            cut_in[at] = cut_out[at]

    def swap_arrival(at, rows):
        @pl.when(jnp.logical_not(home))
        def _():
            swap(at).wait_recv()

        rows[...] = cut_in[at].astype(jnp.float32).reshape(PAIRS, 8, TILE)
        return jnp.concatenate([rows[:, k] for k in range(8)], axis=1)

    cut(mid, 16, 2, 0)
    swap_start(0)

    for copy in o_copies:
        copy.wait_recv()
    for k in range(ROLES):
        w_all[k, yx] = (w_in[k, 0] + w_in[k, 1]) + (w_in[k, 2] + w_in[k, 3])
    w_copies = [send(w_all.at[:, yx], w_all.at[:, yx], wy_sem, d, role, to_spot(to)) for d, to in spots]

    @pl.when(role > 0)
    def _():
        to_above(1).wait_recv()
        out = advance(ext, 1, 16, 64, lane_64)
        for c in range(3):
            mid[c, 1, pl.ds(16, 64)] = out[c]

    @pl.when(role < ROLES - 1)
    def _():
        to_below(1).wait_recv()
        out = advance(ext, 10, 16, 64, lane_64)
        for c in range(3):
            mid[c, 10, pl.ds(16, 64)] = out[c]

    @pl.when(role == 0)
    def _():
        mid[:, 1, pl.ds(16, 64)] = jnp.zeros((3, 64, TILE), jnp.float32)

    @pl.when(role == ROLES - 1)
    def _():
        mid[:, 10, pl.ds(16, 64)] = jnp.zeros((3, 64, TILE), jnp.float32)

    def outer(z, carry):
        out = advance(mid, z, 16, 64, lane_64)
        for c in range(3):
            after_two[c, z - 2] = out[c]
        return carry

    lax.fori_loop(2, 6, outer, 0)
    for copy in later:
        copy.wait()

    a = swap_arrival(0, a_rows)
    a_low = a.astype(jnp.bfloat16)
    bands[team] = pass_(a_low, plane[0], NT) + pass_(a_low, plane[1], NT)
    copies = [send(bands.at[team], bands.at[team], band_sem, d, role, place(to, slab)) for d, to in teams]

    lax.fori_loop(6, 10, outer, 0)
    second_copy = fetch(0, after_two, second_out)
    cut(after_two, 0, 0, 1)
    swap_start(1)

    for copy in copies:
        copy.wait_recv()
    every = jnp.concatenate([bands[b] for b in range(ROLES)], axis=0)
    halves = jnp.concatenate([every[:, :TILE], every[:, TILE:]], axis=0)
    coef = dot3(split(halves), (spread[0], spread[1]), TN)
    for copy in w_copies:
        copy.wait_recv()

    def blocks_out(ref, s, part):
        part = part.reshape(2, 8, 8, TILE)
        for core in range(2):
            ref[s // 2 * 2 + core, pl.ds(s % 2 * 8, 8)] = part[core]

    mixed = []
    for s in range(SH):
        at = (3 * SH + s) * TILE
        blocks_out(a_send, s, coef[:, at : at + TILE])
        total = None
        for i in range(3):
            at = (i * SH + s) * TILE
            weights = jnp.concatenate(
                [w_all[s // 2 * 2 + core, pl.ds(s % 2 * 8, 8), i].reshape(64, TILE) for core in range(2)], axis=0
            )
            term = coef[:, at : at + TILE] * weights
            total = term if total is None else total + term
        mixed.append(total)
    mixed = split(jnp.concatenate(mixed, axis=1))

    def back(to):
        rows = pl.ds(pl.multiple_of(to * 256, 256), 256)
        y_send[to] = dot3((inverse[0, rows], inverse[1, rows]), mixed, NT)

    y_copies = []
    for d, to in (teams[1], teams[0], teams[2]):
        back(to)
        y_copies.append((d, send(y_send.at[to], y_got.at[team], y_sem, d, role, place(to, slab))))
    back(team)
    y_got[team] = y_send[team]
    for k in range(PAIRS):
        out_sum[k] = jnp.zeros((8, AREA), jnp.float32)

    def forward(q):
        rows = jnp.concatenate([y_got[q, :TILE], y_got[q, TILE:]], axis=1)
        slope[q] = dot3(split(rows), (plane[0], plane[1]))
        channels = pl.ds(pl.multiple_of(q * PART, PART), PART)
        by_seen = [seen_wide[i, channels] for i in range(3)]
        by_proj = [proj_wide[j, channels] for j in range(3)]

        def gelu(z, carry):
            at = pl.ds(pl.multiple_of(z * PART, PART), PART)
            for k in range(8):
                lanes = slice(k * TILE, (k + 1) * TILE)
                x = slope[q, at, lanes]
                for i in range(3):
                    x = x + by_seen[i] * a_rows[z * 3 + i, k : k + 1]
                square = x * x
                t = jnp.tanh(x * (root + (root * 0.044715) * square))
                half = 0.5 + 0.5 * t
                value = x * half
                act[q, at, lanes] = value
                slope[q, at, lanes] = half + value * (1.0 - t) * (root + (root * 3.0 * 0.044715) * square)
                for j in range(3):
                    term = by_proj[j] * value
                    out_sum[z * 3 + j, :, lanes] += term[:8] + term[8:]
            return carry

        lax.fori_loop(0, PLANES, gelu, 0)

    forward(team)
    for n, (d, copy) in enumerate(y_copies):
        copy.wait_recv()
        if n == 1:
            a_copies = [send(a_send.at[:, to], a_got.at[yx], a_sem, d, role, to_spot(to)) for d, to in spots]
            a_got[yx] = a_send[:, yx]
        forward((team + ROLES - d) % ROLES)

    wanted = swap_arrival(1, t_rows)
    out = jnp.concatenate([jnp.sum(out_sum[k], axis=0, keepdims=True) for k in range(PAIRS)], axis=0)
    error = a + out - wanted
    doubled = 2.0 * error
    for k in range(8):
        twice[:, k] = doubled[:, k * TILE : (k + 1) * TILE]

    def backward(q):
        channels = pl.ds(pl.multiple_of(q * PART, PART), PART)
        by_proj = [proj_wide[j, channels] for j in range(3)]

        def chain(z, carry):
            at = pl.ds(pl.multiple_of(z * PART, PART), PART)
            for k in range(8):
                lanes = slice(k * TILE, (k + 1) * TILE)
                g = by_proj[0] * twice[z * 3, k : k + 1]
                for j in range(1, 3):
                    g = g + by_proj[j] * twice[z * 3 + j, k : k + 1]
                g = g * slope[q, at, lanes]
                slope[q, at, lanes] = g
                g_high[at, lanes], g_low[at, lanes] = split(g)
            return carry

        lax.fori_loop(0, PLANES, chain, 0)
        g_send[q] = dot3((g_high[...], g_low[...]), (plane[0], plane[1]), NT)

    g_copies = []
    for d, to in (teams[1], teams[0], teams[2]):
        backward(to)
        g_copies.append(send(g_send.at[to], g_got.at[team], g_sem, d, role, place(to, slab)))
    backward(team)
    g_got[team] = g_send[team]

    row_8 = lax.broadcasted_iota(jnp.int32, (8, TILE), 0)
    lane = lax.broadcasted_iota(jnp.int32, (8, TILE), 1)
    zero = jnp.zeros((8, TILE), jnp.float32)
    wide = jnp.zeros((PART, TILE), jnp.float32)

    def cells(q, carry):
        def over(z, sums):
            at = pl.ds(pl.multiple_of(z * PART, PART), PART)
            sums = list(sums)
            for k in range(8):
                lanes = slice(k * TILE, (k + 1) * TILE)
                g, value = slope[q, at, lanes], act[q, at, lanes]
                for i in range(3):
                    sums[i] = sums[i] + g * a_rows[z * 3 + i, k : k + 1]
                    sums[3 + i] = sums[3 + i] + value * twice[z * 3 + i, k : k + 1]
            return tuple(sums)

        return lax.fori_loop(0, PLANES, over, (wide,) * 6)

    by_quarter = [cells(q, 0) for q in range(ROLES)]

    def channel_rows(k, row):
        column = jnp.concatenate([sums[k] for sums in by_quarter], axis=0)
        return dot(jnp.where(row_8 == row, 1.0, 0.0), column, NT)

    cross_rows = sum(channel_rows(i, i) for i in range(3))
    proj_rows = sum(channel_rows(3 + j, j) for j in range(3))
    sse = jnp.sum(error * error, keepdims=True)

    for copy in g_copies:
        copy.wait_recv()
    stacked = jnp.concatenate([g_got[b][:, h * TILE : (h + 1) * TILE] for b in range(ROLES) for h in range(2)], axis=0)
    grad = dot3(split(stacked), (inverse[0], inverse[1]), TN)
    for s in range(SH):
        blocks_out(m_send, s, grad[:, s * TILE : (s + 1) * TILE])
    m_copies = [send(m_send.at[:, to], m_got.at[yx], m_sem, d, role, to_spot(to)) for d, to in spots]
    m_got[yx] = m_send[:, yx]
    for copy in a_copies:
        copy.wait_recv()
    a_all = split(a_got[...].reshape(SLABS * 8, TILE))
    a_all = dot2(a_all, expand[...])
    for i in range(3):
        a_wide[i] = a_all[:, i * TILE : (i + 1) * TILE].reshape(YX, ROLES, 8, TILE)
    for copy in m_copies:
        copy.wait_recv()

    crossed = []
    for b in range(ROLES):
        sums = [zero, zero, zero]
        for k in range(YX):
            g = m_got[k, b]
            sums = [sums[i] + a_wide[i, k, b] * g for i in range(3)]
        crossed.append(jnp.concatenate(sums, axis=1))
    crossed = dot2(split(jnp.concatenate(crossed, axis=0)), sort[...])
    for b in range(ROLES):
        for k in range(ROLES):
            r_send[k, b] = crossed[b * 8 : b * 8 + 8, k * TILE : (k + 1) * TILE]
    r_copies = [
        send(r_send.at[to // ROLES, to % ROLES], r_got.at[role, team], back_sem, d, to // ROLES, place(to % ROLES, slab))
        for d, to in crew
    ]
    r_got[role, team] = r_send[role, team]
    for copy in r_copies:
        copy.wait_recv()
    joined = [(r_got[0, q] + r_got[1, q]) + (r_got[2, q] + r_got[3, q]) for q in range(ROLES)]
    joined = dot2(split(jnp.concatenate(joined, axis=1)), sort[...], NT)
    squares = jnp.zeros((WIDTH, TILE), jnp.float32)
    lift_sum = [jnp.zeros((WIDTH, WIDTH), jnp.float32)] * 3
    for k in range(8):
        rows = [joined[k : k + 1, i * TILE : (i + 1) * TILE] for i in range(3)]
        value = lift_t[:, 0:1] * rows[0] + lift_t[:, 1:2] * rows[1] + lift_t[:, 2:3] * rows[2]
        raw[k] = value
        squares = squares + value * value
        for i in range(3):
            lift_sum[i] = lift_sum[i] + (
                spectral[k] * rows[i][:, :WIDTH] + spectral[8 + k] * rows[i][:, WIDTH:]
            )
    raw_copy = fetch(1, raw, raw_out)
    left = cross_rows
    for i in range(3):
        left = left + dot(jnp.where(row_8[:, :WIDTH] == 3 + i, 1.0, 0.0), lift_sum[i], NT)
    tile = jnp.concatenate([left, proj_rows], axis=1)
    tile = tile + jnp.where((row_8 == 6) & (lane == patch), sse, 0.0)
    tile = tile + jnp.where(row_8 == 7, jnp.sum(squares, keepdims=True), 0.0)

    s_crew[role, team] = tile
    copies = [
        send(s_crew.at[role, team], s_crew.at[role, team], sc_sem, d, to // ROLES, place(to % ROLES, slab))
        for d, to in crew
    ]
    for copy in copies:
        copy.wait_recv()
    s_yx[yx] = jnp.sum(s_crew[...], axis=(0, 1))
    copies = [send(s_yx.at[yx], s_yx.at[yx], sy_sem, d, role, to_spot(to)) for d, to in spots]
    for copy in copies:
        copy.wait_recv()
    tile_out[...] = jnp.sum(s_yx[...], axis=0)

    for copy in pending:
        copy.wait_send()
    second_copy.wait()
    raw_copy.wait()
    to_after.wait_send()
    to_before.wait_send()

    @pl.when(role > 0)
    def _():
        to_below(0).wait_send()
        to_below(1).wait_send()
        corner(False, True, 0).wait_send()
        corner(False, False, 1).wait_send()

    @pl.when(role < ROLES - 1)
    def _():
        to_above(0).wait_send()
        to_above(1).wait_send()
        corner(True, True, 2).wait_send()
        corner(True, False, 3).wait_send()

    @pl.when(jnp.logical_not(home))
    def _():
        swap(0).wait_send()
        swap(1).wait_send()


def result(*shape):
    return jax.ShapeDtypeStruct(shape, jnp.float32)


def step(anchors, velocity, spectral, lift, mix, proj):
    vmem = pl.BlockSpec(memory_space=pltpu.VMEM)
    anywhere = pl.BlockSpec(memory_space=pltpu.HBM)
    dma = pltpu.SemaphoreType.DMA

    def room(*shape):
        return pltpu.VMEM(shape, jnp.float32)

    def narrow(*shape):
        return pltpu.VMEM(shape, jnp.bfloat16)

    return pl.pallas_call(
        step_kernel,
        out_shape=(result(3, PLANES, 64, TILE), result(8, WIDTH, TILE), result(8, TILE)),
        in_specs=[pl.BlockSpec(memory_space=pltpu.SMEM)] + [anywhere] * 10,
        out_specs=(anywhere, anywhere, vmem),
        scratch_shapes=[
            room(3, 12, ROWS, TILE),
            room(3, 12, ROWS, TILE),
            room(3, PLANES, 64, TILE),
            room(MODES, WIDTH, WIDTH),
            room(3, WIDTH),
            room(WIDTH, WIDTH),
            room(3, WIDTH),
            narrow(2, 256, AREA),
            narrow(2, 2 * ROLES * PAIRS, 4 * SH * TILE),
            narrow(2, ROLES * 256, SH * TILE),
            narrow(TILE, 3 * TILE),
            narrow(3 * TILE, ROLES * TILE),
            room(ROLES, 3, 8, TILE),
            room(ROLES, ROLES, 3, 8, TILE),
            room(ROLES, YX, 3, 8, TILE),
            narrow(2, 12, 16, TILE),
            narrow(2, 12, 16, TILE),
            room(PAIRS, 8, TILE),
            room(PAIRS, 8, TILE),
            room(ROLES, PAIRS, 256),
            room(ROLES, YX, 8, TILE),
            room(YX, ROLES, 8, TILE),
            room(3, YX, ROLES, 8, TILE),
            room(ROLES, 256, TILE),
            room(ROLES, 256, TILE),
            room(3, WIDTH, TILE),
            room(3, WIDTH, TILE),
            room(ROLES, TILE, AREA),
            room(ROLES, TILE, AREA),
            narrow(TILE, AREA),
            narrow(TILE, AREA),
            room(PAIRS, 8, AREA),
            room(PAIRS, 8, TILE),
            room(ROLES, TILE, 256),
            room(ROLES, TILE, 256),
            room(ROLES, YX, 8, TILE),
            room(YX, ROLES, 8, TILE),
            room(ROLES, ROLES, 8, TILE),
            room(ROLES, ROLES, 8, TILE),
            room(8, WIDTH, TILE),
            room(ROLES, ROLES, 8, TILE),
            room(YX, 8, TILE),
            dma((10,)),
            dma((2, 4)),
            dma((2, 2)),
            dma((2, 4)),
            dma((2, CREW)),
            dma((2, 2)),
            dma((2, YX)),
            dma((2, ROLES)),
            dma((2, ROLES)),
            dma((2, ROLES)),
            dma((2, YX)),
            dma((2, YX)),
            dma((2, CREW)),
            dma((2, CREW)),
            dma((2, YX)),
        ],
        compiler_params=pltpu.CompilerParams(
            collective_id=0, has_side_effects=True, vmem_limit_bytes=63 * 2**20
        ),
    )(anchors, velocity, spectral, lift, mix, proj, *tables())


def finish_kernel(
    second, raw, tile, lift, mix, table, second_out, loss_out, lift_out, mix_out, proj_out, spec_out, held, copy_sem
):
    fetches = [pltpu.make_async_copy(second.at[c], held.at[c], copy_sem.at[0, c]) for c in range(3)]
    stores = [pltpu.make_async_copy(held.at[c], second_out.at[c], copy_sem.at[1, c]) for c in range(3)]
    for copy in fetches:
        copy.start()

    for get, put in zip(fetches, stores):
        get.wait()
        put.start()

    def normal(total):
        mean = jnp.sum(total * total, keepdims=True) / total.size
        return total / jnp.sqrt(mean + tiny_eps)

    cross = tile[0:3, :WIDTH]
    proj_out[...] = normal(tile[0:3, WIDTH:])
    lift_out[...] = normal(tile[3:6, :WIDTH] + dot(cross, mix[...], NT))
    mix_out[...] = normal(dot(lift[...], cross, TN))
    scale = 1.0 / jnp.sqrt(tile[7:8, 0:1] / (MODES**3 * WIDTH * WIDTH) + tiny_eps)
    for k in range(8):
        value = raw[k] * scale
        spec_out[k] = value[:, :WIDTH]
        spec_out[8 + k] = value[:, WIDTH:]
    losses = tile[6:7, :] / (3.0 * PATCH**3)
    lanes = lax.broadcasted_iota(jnp.int32, (1, TILE), 1)
    found = [jnp.sum(jnp.where(lanes == table[0:1, k : k + 1], losses, 0.0), axis=1, keepdims=True) for k in range(2)]
    loss_out[...] = jnp.concatenate(found, axis=1)
    for copy in stores:
        copy.wait()


def finish(second, raw, tile, lift, mix, table):
    vmem = pl.BlockSpec(memory_space=pltpu.VMEM)
    anywhere = pl.BlockSpec(memory_space=pltpu.HBM)
    return pl.pallas_call(
        finish_kernel,
        out_shape=(
            result(3, PLANES, 64, TILE),
            result(1, 2),
            result(3, WIDTH),
            result(WIDTH, WIDTH),
            result(3, WIDTH),
            result(MODES, WIDTH, WIDTH),
        ),
        in_specs=[anywhere] + [vmem] * 5,
        out_specs=(anywhere,) + (vmem,) * 5,
        scratch_shapes=[pltpu.VMEM((3, PLANES, 64, TILE), jnp.float32), pltpu.SemaphoreType.DMA((2, 3))],
    )(second, raw, tile, lift, mix, table)


def on_device(velocity, anchors, slot_table, lift, mix, proj, spectral):
    second, raw, tile = step(anchors, velocity, spectral, lift, mix, proj)
    return finish(second, raw, tile, lift, mix, slot_table)


def solution(mesh):
    return jax.shard_map(
        on_device,
        mesh=mesh,
        in_specs=(
            P(None, "role", "slab", None),
            P("slab", None),
            P("slab", None),
            P(),
            P(),
            P(),
            P(("role", "slab"), None, None),
        ),
        out_specs=(
            P(None, "role", "slab", None),
            P("slab", None),
            P(),
            P(),
            P(),
            P(("role", "slab"), None, None),
        ),
        check_vma=False,
    )
```

profile of v0, /device:TPU:1, one launch (start us, length us, event | category | flops | bytes accessed | tf_op | source)
XLA Modules:
  0.0 88.0 jit_solution(16339507756505129923)
XLA Ops:
  0.6 83.7 %shard_map.163 = (f32[3,8,64,128]{3,2,1,0:T(8,128)}, f32[8,64,128]{2,1,0:T(8,128)}, f32[8,128]{1,0:T(8,128)}) custom-call(s32[1,2]{1,0:T(1,128)} %anchors.1, f32[3,8,64,128]{3,2,1,0:T(8,128)} %vel.1, f32[16,64,64]{2,1,0:T(8,128)} %spectral_in.1, f32[3,64]{1,0:T(4,128)} %lift.1, f32[64,64]{1,0:T(8,128)} %mix.1, f32[3,64]{1,0:T(4,128)} %proj_in.1, ...), custom_call_target="tpu_custom_call" | custom-call | tf_op jit(solution)/shard_map/pallas_call | solution.py:659
  84.3 3.7 %shard_map.164 = (f32[3,8,64,128]{3,2,1,0:T(8,128)}, f32[1,2]{1,0:T(1,128)}, f32[3,64]{1,0:T(4,128)}, f32[64,64]{1,0:T(8,128)}, f32[3,64]{1,0:T(4,128)}, /*index=5*/f32[16,64,64]{2,1,0:T(8,128)}) custom-call(f32[3,8,64,128]{3,2,1,0:T(8,128)} %get-tuple-element.9.second, f32[8,64,128]{2,1,0:T(8,128)} %get-tuple-element.10.raw, ...), custom_call_target="tpu_custom_call" | custom-call | tf_op jit(solution)/shard_map/pallas_call | solution.py:765
where the time goes:
time: 88.2 us; the launch traced here: 88 us
  Pallas kernels  87.4 us (99%)
    pallas_call x1, Pallas kernels, step(): pl.pallas_call(step_kernel, out_shape=(result(3, PLANES, 64, TILE), resul...  83.7 us
    pallas_call x1, Pallas kernels, finish(): pl.pallas_call(finish_kernel, out_shape=(result(3, PLANES, 64, TILE), res...  3.67 us

commit v1 on v0

--- a/solution.py
+++ b/solution.py
@@ -98,7 +98,7 @@
     anchors, vel, spectral_in, lift_in, mix_in, proj_in, plane_in, spread_in, inverse_in, expand_in, sort_in,
     second_out, raw_out, tile_out,
     ext, mid, after_two, spectral, lift, mix, proj, plane, spread, inverse, expand, sort,
-    w_send, w_in, w_all, cut_out, cut_in, a_rows, t_rows, bands, a_send, a_got, a_wide, y_send, y_got,
+    w_send, w_in, w_all, cut_out, cut_in, a_rows, t_rows, band, bands, a_send, a_got, a_wide, y_send, y_got,
     seen_wide, proj_wide, act, slope, g_high, g_low, out_sum, twice, g_send, g_got, m_send, m_got, r_send, r_got, raw,
     s_crew, s_yx,
     local_sem, z_sem, x_sem, c_sem, cross_sem, swap_sem, wy_sem, band_sem, y_sem, g_sem, a_sem, m_sem, back_sem,
@@ -136,10 +136,12 @@
         return copy
 
     own = fetch(0, vel, ext.at[:, pl.ds(2, PLANES), pl.ds(16, 64)])
-    fetched = [fetch(1, spectral_in, spectral), fetch(2, lift_in, lift), fetch(3, mix_in, mix), fetch(4, proj_in, proj)]
+    fetched = [
+        fetch(1, spectral_in, spectral), fetch(2, lift_in, lift), fetch(3, mix_in, mix), fetch(4, proj_in, proj),
+        fetch(9, sort_in, sort),
+    ]
     later = [
-        fetch(5, plane_in, plane), fetch(6, spread_in, spread), fetch(7, inverse_in, inverse), fetch(8, expand_in, expand),
-        fetch(9, sort_in, sort),
+        fetch(5, plane_in, plane), fetch(6, spread_in, spread), fetch(7, inverse_in, inverse), fetch(8, expand_in, expand)
     ]
 
     barrier = pltpu.get_barrier_semaphore()
@@ -165,15 +167,6 @@
     for _, to in spots:
         greet(role, to_spot(to))
 
-    source = lax.broadcasted_iota(jnp.int32, (ROLES * TILE, TILE), 0)
-    target = lax.broadcasted_iota(jnp.int32, (ROLES * TILE, TILE), 1)
-    pick = (
-        (source // TILE == target % WIDTH // PART)
-        & (source % TILE // WIDTH == target // WIDTH)
-        & (source % WIDTH // PART == role)
-        & (source % PART == target % PART)
-    )
-    pick = jnp.where(pick, 1.0, 0.0).astype(jnp.bfloat16)
     for copy in fetched:
         copy.wait()
     row_ky = lax.broadcasted_iota(jnp.int32, (MODES, MODES * WIDTH), 0)
@@ -185,10 +178,10 @@
         split(jnp.concatenate(blocks, axis=0)), split(spectral[...].reshape(MODES * WIDTH, WIDTH))
     )
     lifted = lifted.reshape(3, 2, 8, WIDTH)
-    lifted = jnp.concatenate([lifted[:, 0].reshape(24, WIDTH), lifted[:, 1].reshape(24, WIDTH)], axis=1)
-    lifted = dot2(split(lifted), pick, NT)
+    lifted = jnp.concatenate([lifted[i, h] for i in range(3) for h in range(2)], axis=1)
+    lifted = dot2(split(lifted), sort[...])
     for k in range(ROLES):
-        w_send[k] = lifted[:, k * TILE : (k + 1) * TILE].reshape(3, 8, TILE)
+        w_send[k] = lifted[:, k * TILE : (k + 1) * TILE]
 
     pl.semaphore_wait(barrier, 34 + 2 * ((role + 1) // 2 % 2))
 
@@ -224,14 +217,10 @@
     @pl.when(role > 0)
     def _():
         to_below(0).start()
-        corner(False, True, 0).start()
-        corner(False, False, 1).start()
 
     @pl.when(role < ROLES - 1)
     def _():
         to_above(0).start()
-        corner(True, True, 2).start()
-        corner(True, False, 3).start()
 
     to_after.start()
     to_before.start()
@@ -245,10 +234,14 @@
     @pl.when(role > 0)
     def _():
         to_below(1).start()
+        corner(False, True, 0).start()
+        corner(False, False, 1).start()
 
     @pl.when(role < ROLES - 1)
     def _():
         to_above(1).start()
+        corner(True, True, 2).start()
+        corner(True, False, 3).start()
 
     @pl.when(role == 0)
     def _():
@@ -270,6 +263,7 @@
 
     lane_80 = lax.broadcasted_iota(jnp.int32, (80, TILE), 1)
     lane_64 = lax.broadcasted_iota(jnp.int32, (64, TILE), 1)
+    lane_8 = lax.broadcasted_iota(jnp.int32, (8, TILE), 1)
 
     def advance(field, z, row, count, lane):
         centre = [field[c, z, pl.ds(row, count)] for c in range(3)]
@@ -299,20 +293,28 @@
 
     lax.fori_loop(3, 9, inner, 0)
 
+    for copy in o_copies:
+        copy.wait_recv()
+    lifted = [jnp.concatenate([w_in[k, r] for r in range(ROLES)], axis=1) for k in range(ROLES)]
+    lifted = dot2(split(jnp.concatenate(lifted, axis=0)), sort[...], NT)
+    for k in range(ROLES):
+        for i in range(3):
+            w_all[k, yx, i] = lifted[k * 8 : k * 8 + 8, i * TILE : (i + 1) * TILE]
+    w_copies = [send(w_all.at[:, yx], w_all.at[:, yx], wy_sem, d, role, to_spot(to)) for d, to in spots]
+
     @pl.when(role > 0)
     def _():
         to_above(0).wait_recv()
-        corner(True, True, 2).wait_recv()
-        corner(True, False, 3).wait_recv()
 
     @pl.when(role < ROLES - 1)
     def _():
         to_below(0).wait_recv()
-        corner(False, True, 0).wait_recv()
-        corner(False, False, 1).wait_recv()
-
-    inner(2, 0)
-    inner(9, 0)
+
+    for z in (2, 9):
+        out = advance(ext, z, 16, 64, lane_64)
+        for c in range(3):
+            mid[c, z, pl.ds(16, 64)] = out[c]
+
 
     x_at, y_at = anchors[0, 0], anchors[0, 1]
     from_lane = lax.broadcasted_iota(jnp.int32, (TILE, TILE), 0)
@@ -357,17 +359,36 @@
         return jnp.concatenate([rows[:, k] for k in range(8)], axis=1)
 
     cut(mid, 16, 2, 0)
+
+    t_rows[...] = cut_out[0].astype(jnp.float32).reshape(PAIRS, 8, TILE)
+    cells_here = jnp.concatenate([t_rows[:, k] for k in range(8)], axis=1).astype(jnp.bfloat16)
+    for copy in later:
+        copy.wait()
+    band[...] = pass_(cells_here, plane[0], NT) + pass_(cells_here, plane[1], NT)
+
+    def band_copy(k):
+        return remote(band, bands.at[role], band_sem.at[0, k], band_sem.at[1, role], team, place(k, slab))
+
+    def band_arrival(k):
+        return remote(band, bands.at[k], band_sem.at[0, k], band_sem.at[1, k], team, place(k, slab))
+
+    for k in range(ROLES):
+
+        @pl.when(jnp.logical_not(home & (k == role)))
+        def _():
+            band_copy(k).start()
+
+    @pl.when(home)
+    def _():
+        bands[role] = band[...]
+
     swap_start(0)
 
-    for copy in o_copies:
-        copy.wait_recv()
-    for k in range(ROLES):
-        w_all[k, yx] = (w_in[k, 0] + w_in[k, 1]) + (w_in[k, 2] + w_in[k, 3])
-    w_copies = [send(w_all.at[:, yx], w_all.at[:, yx], wy_sem, d, role, to_spot(to)) for d, to in spots]
-
     @pl.when(role > 0)
     def _():
         to_above(1).wait_recv()
+        corner(True, True, 2).wait_recv()
+        corner(True, False, 3).wait_recv()
         out = advance(ext, 1, 16, 64, lane_64)
         for c in range(3):
             mid[c, 1, pl.ds(16, 64)] = out[c]
@@ -375,9 +396,17 @@
     @pl.when(role < ROLES - 1)
     def _():
         to_below(1).wait_recv()
+        corner(False, True, 0).wait_recv()
+        corner(False, False, 1).wait_recv()
         out = advance(ext, 10, 16, 64, lane_64)
         for c in range(3):
             mid[c, 10, pl.ds(16, 64)] = out[c]
+
+    for z in (2, 9):
+        for row in (8, 80):
+            out = advance(ext, z, row, 8, lane_8)
+            for c in range(3):
+                mid[c, z, pl.ds(row, 8)] = out[c]
 
     @pl.when(role == 0)
     def _():
@@ -394,21 +423,17 @@
         return carry
 
     lax.fori_loop(2, 6, outer, 0)
-    for copy in later:
-        copy.wait()
-
-    a = swap_arrival(0, a_rows)
-    a_low = a.astype(jnp.bfloat16)
-    bands[team] = pass_(a_low, plane[0], NT) + pass_(a_low, plane[1], NT)
-    copies = [send(bands.at[team], bands.at[team], band_sem, d, role, place(to, slab)) for d, to in teams]
-
     lax.fori_loop(6, 10, outer, 0)
     second_copy = fetch(0, after_two, second_out)
     cut(after_two, 0, 0, 1)
     swap_start(1)
 
-    for copy in copies:
-        copy.wait_recv()
+    for k in range(ROLES):
+
+        @pl.when(jnp.logical_not(home & (k == role)))
+        def _():
+            band_arrival(k).wait_recv()
+
     every = jnp.concatenate([bands[b] for b in range(ROLES)], axis=0)
     halves = jnp.concatenate([every[:, :TILE], every[:, TILE:]], axis=0)
     coef = dot3(split(halves), (spread[0], spread[1]), TN)
@@ -445,6 +470,7 @@
         y_copies.append((d, send(y_send.at[to], y_got.at[team], y_sem, d, role, place(to, slab))))
     back(team)
     y_got[team] = y_send[team]
+    a = swap_arrival(0, a_rows)
     for k in range(PAIRS):
         out_sum[k] = jnp.zeros((8, AREA), jnp.float32)
 
@@ -635,6 +661,12 @@
         corner(True, True, 2).wait_send()
         corner(True, False, 3).wait_send()
 
+    for k in range(ROLES):
+
+        @pl.when(jnp.logical_not(home & (k == role)))
+        def _():
+            band_copy(k).wait_send()
+
     @pl.when(jnp.logical_not(home))
     def _():
         swap(0).wait_send()
@@ -674,13 +706,14 @@
             narrow(2, ROLES * 256, SH * TILE),
             narrow(TILE, 3 * TILE),
             narrow(3 * TILE, ROLES * TILE),
-            room(ROLES, 3, 8, TILE),
-            room(ROLES, ROLES, 3, 8, TILE),
+            room(ROLES, 8, TILE),
+            room(ROLES, ROLES, 8, TILE),
             room(ROLES, YX, 3, 8, TILE),
             narrow(2, 12, 16, TILE),
             narrow(2, 12, 16, TILE),
             room(PAIRS, 8, TILE),
             room(PAIRS, 8, TILE),
+            room(PAIRS, 256),
             room(ROLES, PAIRS, 256),
             room(ROLES, YX, 8, TILE),
             room(YX, ROLES, 8, TILE),

time: 88.2 us -> 85.1 us (0.965)
  Pallas kernels: 87.4 us -> 84.4 us
    pallas_call x1, Pallas kernels: 83.7 us -> 80.7 us  [step(): pl.pallas_call(step_kernel, out_shape=(result(3, PLANES, 64, TILE), resul...]
where the time goes in v1:
time: 85.1 us; the launch traced here: 85 us
  Pallas kernels  84.4 us (99%)
    pallas_call x1, Pallas kernels, step(): pl.pallas_call(step_kernel, out_shape=(result(3, PLANES, 64, TILE), resul...  80.7 us
    pallas_call x1, Pallas kernels, finish(): pl.pallas_call(finish_kernel, out_shape=(result(3, PLANES, 64, TILE), res...  3.67 us

profile of v1, /device:TPU:1, one launch (start us, length us, event | category | flops | bytes accessed | tf_op | source)
XLA Modules:
  0.0 85.0 jit_solution(1723064887730366727)
XLA Ops:
  0.6 80.7 %shard_map.163 = (f32[3,8,64,128]{3,2,1,0:T(8,128)}, f32[8,64,128]{2,1,0:T(8,128)}, f32[8,128]{1,0:T(8,128)}) custom-call(s32[1,2]{1,0:T(1,128)} %anchors.1, f32[3,8,64,128]{3,2,1,0:T(8,128)} %vel.1, f32[16,64,64]{2,1,0:T(8,128)} %spectral_in.1, f32[3,64]{1,0:T(4,128)} %lift.1, f32[64,64]{1,0:T(8,128)} %mix.1, f32[3,64]{1,0:T(4,128)} %proj_in.1, ...), custom_call_target="tpu_custom_call" | custom-call | tf_op jit(solution)/shard_map/pallas_call | solution.py:691
  81.3 3.7 %shard_map.164 = (f32[3,8,64,128]{3,2,1,0:T(8,128)}, f32[1,2]{1,0:T(1,128)}, f32[3,64]{1,0:T(4,128)}, f32[64,64]{1,0:T(8,128)}, f32[3,64]{1,0:T(4,128)}, /*index=5*/f32[16,64,64]{2,1,0:T(8,128)}) custom-call(f32[3,8,64,128]{3,2,1,0:T(8,128)} %get-tuple-element.9.second, f32[8,64,128]{2,1,0:T(8,128)} %get-tuple-element.10.raw, ...), custom_call_target="tpu_custom_call" | custom-call | tf_op jit(solution)/shard_map/pallas_call | solution.py:798

commit v2 on v1

--- a/solution.py
+++ b/solution.py
@@ -84,7 +84,7 @@
     expand = np.pad(expand, ((0, TILE - 24), (0, 0)))
     sort = np.einsum("ij,hg,rs,cd->ihrcsjgd", eye3, eye2, eye4, eye16).reshape(3 * TILE, ROLES, 96)
     sort = np.pad(sort, ((0, 0), (0, 0), (0, TILE - 96))).reshape(3 * TILE, ROLES * TILE)
-    return [pair(plane), pair(np.concatenate([spread, short], axis=1)), pair(inverse), jnp.asarray(expand, jnp.bfloat16), jnp.asarray(sort, jnp.bfloat16)]
+    return [pair(plane), pair(plane.T), pair(np.concatenate([spread, short], axis=1)), pair(inverse), jnp.asarray(expand, jnp.bfloat16), jnp.asarray(sort, jnp.bfloat16)]
 
 
 def place(team, slab):
@@ -95,9 +95,9 @@
 
 
 def step_kernel(
-    anchors, vel, spectral_in, lift_in, mix_in, proj_in, plane_in, spread_in, inverse_in, expand_in, sort_in,
+    anchors, vel, spectral_in, lift_in, mix_in, proj_in, plane_in, across_in, spread_in, inverse_in, expand_in, sort_in,
     second_out, raw_out, tile_out,
-    ext, mid, after_two, spectral, lift, mix, proj, plane, spread, inverse, expand, sort,
+    ext, mid, after_two, spectral, lift, mix, proj, plane, across, spread, inverse, expand, sort,
     w_send, w_in, w_all, cut_out, cut_in, a_rows, t_rows, band, bands, a_send, a_got, a_wide, y_send, y_got,
     seen_wide, proj_wide, act, slope, g_high, g_low, out_sum, twice, g_send, g_got, m_send, m_got, r_send, r_got, raw,
     s_crew, s_yx,
@@ -141,7 +141,7 @@
         fetch(9, sort_in, sort),
     ]
     later = [
-        fetch(5, plane_in, plane), fetch(6, spread_in, spread), fetch(7, inverse_in, inverse), fetch(8, expand_in, expand)
+        fetch(5, plane_in, plane), fetch(10, across_in, across), fetch(6, spread_in, spread), fetch(7, inverse_in, inverse), fetch(8, expand_in, expand)
     ]
 
     barrier = pltpu.get_barrier_semaphore()
@@ -185,6 +185,12 @@
 
     pl.semaphore_wait(barrier, 34 + 2 * ((role + 1) // 2 % 2))
 
+    o_copies = [
+        send(w_send.at[to % ROLES], w_in.at[team, role], cross_sem, d, to // ROLES, place(to % ROLES, slab))
+        for d, to in crew
+    ]
+    w_in[team, role] = w_send[team]
+
     def to_below(k):
         return remote(
             vel.at[:, pl.ds(k, 1)], ext.at[:, pl.ds(10 + k, 1), pl.ds(16, 64)],
@@ -224,12 +230,6 @@
 
     to_after.start()
     to_before.start()
-
-    o_copies = [
-        send(w_send.at[to % ROLES], w_in.at[team, role], cross_sem, d, to // ROLES, place(to % ROLES, slab))
-        for d, to in crew
-    ]
-    w_in[team, role] = w_send[team]
 
     @pl.when(role > 0)
     def _():
@@ -364,7 +364,7 @@
     cells_here = jnp.concatenate([t_rows[:, k] for k in range(8)], axis=1).astype(jnp.bfloat16)
     for copy in later:
         copy.wait()
-    band[...] = pass_(cells_here, plane[0], NT) + pass_(cells_here, plane[1], NT)
+    band[...] = pass_(cells_here, across[0], NN) + pass_(cells_here, across[1], NN)
 
     def band_copy(k):
         return remote(band, bands.at[role], band_sem.at[0, k], band_sem.at[1, role], team, place(k, slab))
@@ -458,11 +458,11 @@
             term = coef[:, at : at + TILE] * weights
             total = term if total is None else total + term
         mixed.append(total)
-    mixed = split(jnp.concatenate(mixed, axis=1))
+    mixed = split(jnp.concatenate([part.T for part in mixed], axis=0))
 
     def back(to):
         rows = pl.ds(pl.multiple_of(to * 256, 256), 256)
-        y_send[to] = dot3((inverse[0, rows], inverse[1, rows]), mixed, NT)
+        y_send[to] = dot3((inverse[0, rows], inverse[1, rows]), mixed)
 
     y_copies = []
     for d, to in (teams[1], teams[0], teams[2]):
@@ -533,7 +533,7 @@
             return carry
 
         lax.fori_loop(0, PLANES, chain, 0)
-        g_send[q] = dot3((g_high[...], g_low[...]), (plane[0], plane[1]), NT)
+        g_send[q] = dot3((g_high[...], g_low[...]), (across[0], across[1]))
 
     g_copies = []
     for d, to in (teams[1], teams[0], teams[2]):
@@ -691,7 +691,7 @@
     return pl.pallas_call(
         step_kernel,
         out_shape=(result(3, PLANES, 64, TILE), result(8, WIDTH, TILE), result(8, TILE)),
-        in_specs=[pl.BlockSpec(memory_space=pltpu.SMEM)] + [anywhere] * 10,
+        in_specs=[pl.BlockSpec(memory_space=pltpu.SMEM)] + [anywhere] * 11,
         out_specs=(anywhere, anywhere, vmem),
         scratch_shapes=[
             room(3, 12, ROWS, TILE),
@@ -702,6 +702,7 @@
             room(WIDTH, WIDTH),
             room(3, WIDTH),
             narrow(2, 256, AREA),
+            narrow(2, AREA, 256),
             narrow(2, 2 * ROLES * PAIRS, 4 * SH * TILE),
             narrow(2, ROLES * 256, SH * TILE),
             narrow(TILE, 3 * TILE),
@@ -737,7 +738,7 @@
             room(8, WIDTH, TILE),
             room(ROLES, ROLES, 8, TILE),
             room(YX, 8, TILE),
-            dma((10,)),
+            dma((11,)),
             dma((2, 4)),
             dma((2, 2)),
             dma((2, 4)),

time: 85.1 us -> 79.5 us (0.934)
  Pallas kernels: 84.4 us -> 78.8 us
    pallas_call x1, Pallas kernels: 80.7 us -> 75.1 us  [step(): pl.pallas_call(step_kernel, out_shape=(result(3, PLANES, 64, TILE), resul...]
where the time goes in v2:
time: 79.5 us; the launch traced here: 79.4 us
  Pallas kernels  78.8 us (99%)
    pallas_call x1, Pallas kernels, step(): pl.pallas_call(step_kernel, out_shape=(result(3, PLANES, 64, TILE), resul...  75.1 us
    pallas_call x1, Pallas kernels, finish(): pl.pallas_call(finish_kernel, out_shape=(result(3, PLANES, 64, TILE), res...  3.67 us

profile of v2, /device:TPU:1, one launch (start us, length us, event | category | flops | bytes accessed | tf_op | source)
XLA Modules:
  0.0 79.4 jit_solution(14353596440426247209)
XLA Ops:
  0.6 75.1 %shard_map.172 = (f32[3,8,64,128]{3,2,1,0:T(8,128)}, f32[8,64,128]{2,1,0:T(8,128)}, f32[8,128]{1,0:T(8,128)}) custom-call(s32[1,2]{1,0:T(1,128)} %anchors.1, f32[3,8,64,128]{3,2,1,0:T(8,128)} %vel.1, f32[16,64,64]{2,1,0:T(8,128)} %spectral_in.1, f32[3,64]{1,0:T(4,128)} %lift.1, f32[64,64]{1,0:T(8,128)} %mix.1, f32[3,64]{1,0:T(4,128)} %proj_in.1, ...), custom_call_target="tpu_custom_call" | custom-call | tf_op jit(solution)/shard_map/pallas_call | solution.py:691
  75.7 3.7 %shard_map.173 = (f32[3,8,64,128]{3,2,1,0:T(8,128)}, f32[1,2]{1,0:T(1,128)}, f32[3,64]{1,0:T(4,128)}, f32[64,64]{1,0:T(8,128)}, f32[3,64]{1,0:T(4,128)}, /*index=5*/f32[16,64,64]{2,1,0:T(8,128)}) custom-call(f32[3,8,64,128]{3,2,1,0:T(8,128)} %get-tuple-element.9.second, f32[8,64,128]{2,1,0:T(8,128)} %get-tuple-element.10.raw, ...), custom_call_target="tpu_custom_call" | custom-call | tf_op jit(solution)/shard_map/pallas_call | solution.py:799

commit v3 on v2

--- a/solution.py
+++ b/solution.py
@@ -109,7 +109,7 @@
     team = slab // 32 * 2 + slab % 2
     patch = role // 2 * 32 + yx * 2 + role % 2
     after, before = (slab + 1) % SLABS, (slab + SLABS - 1) % SLABS
-    teams = [(d, (team + d) % ROLES) for d in range(1, ROLES)]
+    teams = {1: team + 1 - 2 * (team % 2), 2: (team + 2) % ROLES, 3: ROLES - 1 - team}
     crew = [(d, (role * ROLES + team + d) % CREW) for d in range(1, CREW)]
     spots = [(d, (yx + d) % YX) for d in range(1, YX)]
     home = role == team
@@ -464,10 +464,11 @@
         rows = pl.ds(pl.multiple_of(to * 256, 256), 256)
         y_send[to] = dot3((inverse[0, rows], inverse[1, rows]), mixed)
 
-    y_copies = []
-    for d, to in (teams[1], teams[0], teams[2]):
+    y_copies = {}
+    for d in (2, 3, 1):
+        to = teams[d]
         back(to)
-        y_copies.append((d, send(y_send.at[to], y_got.at[team], y_sem, d, role, place(to, slab))))
+        y_copies[d] = send(y_send.at[to], y_got.at[team], y_sem, d, role, place(to, slab))
     back(team)
     y_got[team] = y_send[team]
     a = swap_arrival(0, a_rows)
@@ -502,12 +503,12 @@
         lax.fori_loop(0, PLANES, gelu, 0)
 
     forward(team)
-    for n, (d, copy) in enumerate(y_copies):
-        copy.wait_recv()
-        if n == 1:
+    for d in (1, 2, 3):
+        y_copies[d].wait_recv()
+        if d == 2:
             a_copies = [send(a_send.at[:, to], a_got.at[yx], a_sem, d, role, to_spot(to)) for d, to in spots]
             a_got[yx] = a_send[:, yx]
-        forward((team + ROLES - d) % ROLES)
+        forward(teams[d])
 
     wanted = swap_arrival(1, t_rows)
     out = jnp.concatenate([jnp.sum(out_sum[k], axis=0, keepdims=True) for k in range(PAIRS)], axis=0)
@@ -536,7 +537,8 @@
         g_send[q] = dot3((g_high[...], g_low[...]), (across[0], across[1]))
 
     g_copies = []
-    for d, to in (teams[1], teams[0], teams[2]):
+    for d in (2, 3, 1):
+        to = teams[d]
         backward(to)
         g_copies.append(send(g_send.at[to], g_got.at[team], g_sem, d, role, place(to, slab)))
     backward(team)

time: 79.5 us -> 80.1 us (level)
  no operation moved by 1% of the time
where the time goes in v3:
time: 80.1 us; the launch traced here: 80 us
  Pallas kernels  79.4 us (99%)
    pallas_call x1, Pallas kernels, step(): pl.pallas_call(step_kernel, out_shape=(result(3, PLANES, 64, TILE), resul...  75.7 us
    pallas_call x1, Pallas kernels, finish(): pl.pallas_call(finish_kernel, out_shape=(result(3, PLANES, 64, TILE), res...  3.67 us

profile of v3, /device:TPU:1, one launch (start us, length us, event | category | flops | bytes accessed | tf_op | source)
XLA Modules:
  0.0 80.0 jit_solution(9818837120208964166)
XLA Ops:
  0.6 75.7 %shard_map.172 = (f32[3,8,64,128]{3,2,1,0:T(8,128)}, f32[8,64,128]{2,1,0:T(8,128)}, f32[8,128]{1,0:T(8,128)}) custom-call(s32[1,2]{1,0:T(1,128)} %anchors.1, f32[3,8,64,128]{3,2,1,0:T(8,128)} %vel.1, f32[16,64,64]{2,1,0:T(8,128)} %spectral_in.1, f32[3,64]{1,0:T(4,128)} %lift.1, f32[64,64]{1,0:T(8,128)} %mix.1, f32[3,64]{1,0:T(4,128)} %proj_in.1, ...), custom_call_target="tpu_custom_call" | custom-call | tf_op jit(solution)/shard_map/pallas_call | solution.py:693
  76.3 3.7 %shard_map.173 = (f32[3,8,64,128]{3,2,1,0:T(8,128)}, f32[1,2]{1,0:T(1,128)}, f32[3,64]{1,0:T(4,128)}, f32[64,64]{1,0:T(8,128)}, f32[3,64]{1,0:T(4,128)}, /*index=5*/f32[16,64,64]{2,1,0:T(8,128)}) custom-call(f32[3,8,64,128]{3,2,1,0:T(8,128)} %get-tuple-element.9.second, f32[8,64,128]{2,1,0:T(8,128)} %get-tuple-element.10.raw, ...), custom_call_target="tpu_custom_call" | custom-call | tf_op jit(solution)/shard_map/pallas_call | solution.py:801

commit v4 on v2

--- a/solution.py
+++ b/solution.py
@@ -502,11 +502,10 @@
         lax.fori_loop(0, PLANES, gelu, 0)
 
     forward(team)
-    for n, (d, copy) in enumerate(y_copies):
+    a_copies = [send(a_send.at[:, to], a_got.at[yx], a_sem, d, role, to_spot(to)) for d, to in spots]
+    a_got[yx] = a_send[:, yx]
+    for d, copy in y_copies:
         copy.wait_recv()
-        if n == 1:
-            a_copies = [send(a_send.at[:, to], a_got.at[yx], a_sem, d, role, to_spot(to)) for d, to in spots]
-            a_got[yx] = a_send[:, yx]
         forward((team + ROLES - d) % ROLES)
 
     wanted = swap_arrival(1, t_rows)

time: 79.5 us -> 79 us (level)
  no operation moved by 1% of the time
where the time goes in v4:
time: 79 us; the launch traced here: 78.8 us
  Pallas kernels  78.2 us (99%)
    pallas_call x1, Pallas kernels, step(): pl.pallas_call(step_kernel, out_shape=(result(3, PLANES, 64, TILE), resul...  74.5 us
    pallas_call x1, Pallas kernels, finish(): pl.pallas_call(finish_kernel, out_shape=(result(3, PLANES, 64, TILE), res...  3.67 us

profile of v4, /device:TPU:1, one launch (start us, length us, event | category | flops | bytes accessed | tf_op | source)
XLA Modules:
  0.0 78.8 jit_solution(3135026779973366825)
XLA Ops:
  0.6 74.5 %shard_map.172 = (f32[3,8,64,128]{3,2,1,0:T(8,128)}, f32[8,64,128]{2,1,0:T(8,128)}, f32[8,128]{1,0:T(8,128)}) custom-call(s32[1,2]{1,0:T(1,128)} %anchors.1, f32[3,8,64,128]{3,2,1,0:T(8,128)} %vel.1, f32[16,64,64]{2,1,0:T(8,128)} %spectral_in.1, f32[3,64]{1,0:T(4,128)} %lift.1, f32[64,64]{1,0:T(8,128)} %mix.1, f32[3,64]{1,0:T(4,128)} %proj_in.1, ...), custom_call_target="tpu_custom_call" | custom-call | tf_op jit(solution)/shard_map/pallas_call | solution.py:690
  75.2 3.7 %shard_map.173 = (f32[3,8,64,128]{3,2,1,0:T(8,128)}, f32[1,2]{1,0:T(1,128)}, f32[3,64]{1,0:T(4,128)}, f32[64,64]{1,0:T(8,128)}, f32[3,64]{1,0:T(4,128)}, /*index=5*/f32[16,64,64]{2,1,0:T(8,128)}) custom-call(f32[3,8,64,128]{3,2,1,0:T(8,128)} %get-tuple-element.9.second, f32[8,64,128]{2,1,0:T(8,128)} %get-tuple-element.10.raw, ...), custom_call_target="tpu_custom_call" | custom-call | tf_op jit(solution)/shard_map/pallas_call | solution.py:798
